TPU v7x, 512 devices: a whole 4x4x16 slice. The times are simulated.
512 devices in a mesh: dp: 4 (over y), blk: 16 (over z_lo, x), uly: 8 (over z_hi, core).
Axes of the slice: x: 4, y: 4, z: 16 (z_hi: 4, z_lo: 4; z = z_hi * 4 + z_lo), core: 2. Of those that a mesh axis runs over, the one named last changes fastest.
Arguments:
- queries: bfloat16 [4, 16384, 4096], P('dp', ('blk', 'uly')), may hold values from -6 to 6
- keys: bfloat16 [4, 16384, 512], P('dp', ('blk', 'uly')), may hold values from -6 to 6
- values: bfloat16 [4, 16384, 512], P('dp', ('blk', 'uly')), may hold values from -6 to 6
- output_gradient: bfloat16 [4, 16384, 4096], P('dp', ('blk', 'uly')), may hold values from -6 to 6
- layer_input: bfloat16 [4, 16384, 8192], P('dp', ('blk', 'uly')), may hold values from -6 to 6
- saved_log_total: float32 [4, 32, 16384], P('dp', 'uly', 'blk'), may hold values from 4 to 7
- row_dot_products: float32 [4, 32, 16384], P('dp', 'uly', 'blk'), may hold values from -6 to 6
- segment_ids: int32 [4, 16384], P('dp'), may hold values from 0 to 63, never falling along the last dimension, each value on 1 to 384 neighbouring positions
- tenants: int32 [4], P('dp'), may hold values from 0 to 3
- adapter_down: bfloat16 [4, 8192, 16], P(None, ('blk', 'uly')), may hold values from -0.0625 to 0.0625
- adapter_up: bfloat16 [4, 16, 4096], P(None, None, 'uly'), may hold values from -1.5 to 1.5
Outputs:
- key_grad: bfloat16 [4, 16384, 512], P('dp', ('blk', 'uly'))
- value_grad: bfloat16 [4, 16384, 512], P('dp', ('blk', 'uly'))
- down_grad: float32 [4, 8192, 16], P(None, ('blk', 'uly'))
- up_grad: float32 [4, 16, 4096], P(None, None, 'uly')
Inputs may be any that keep to these rules, and one draw needn't show every extreme that they name: `segment_ids`: documents are runs of consecutive tokens numbered in order. `tenants`: several sequences may use one adapter.
All inputs are finite; a program needn't handle non-finite values.
Results may differ from a plain program's by a relative error of at most 0.012.
Values may be sent and summed in bfloat16 or wider, within the bound.
A program may use at most 64 MiB of HBM per device.

v0:
```python
import jax
import jax.numpy as jnp
from jax import lax
from jax.sharding import PartitionSpec as P

HEAD_SIZE = 128
QUERY_HEADS = 32
KEY_VALUE_HEADS = 4
TEN = 4


ADAPTER_SCALE = 2.0


def shifted(value, axis, steps):
    count = lax.axis_size(axis)
    first, last = (max(0, -steps), min(count, count - steps))
    return lax.ppermute(value, axis, [(source, source + steps) for source in range(first, last)])


def tile_grads(q_s, g_s, lse_s, dots_s, k_s, v_s, allowed, scale):
    f32 = jnp.float32
    scores = jnp.einsum("rkgd,ckd->kgrc", q_s, k_s, preferred_element_type=f32) * scale
    probs = jnp.where(allowed, jnp.exp(scores - lse_s[..., None]), 0.0)
    probs_low = probs.astype(jnp.bfloat16)
    value_part = jnp.einsum("kgrc,rkgd->ckd", probs_low, g_s, preferred_element_type=f32)
    prob_grad = jnp.einsum("rkgd,ckd->kgrc", g_s, v_s, preferred_element_type=f32)
    score_grad = (probs * (prob_grad - dots_s[..., None])).astype(jnp.bfloat16)
    query_part = jnp.einsum("kgrc,ckd->rkgd", score_grad, k_s, preferred_element_type=f32) * scale
    key_part = jnp.einsum("kgrc,rkgd->ckd", score_grad, q_s, preferred_element_type=f32) * scale
    return (query_part, key_part, value_part)


def match(first_ids, second_ids):
    return first_ids[:, None] == second_ids[None, :]


def local(
    queries,
    keys,
    values,
    output_gradient,
    layer_input,
    saved_log_total,
    row_dot_products,
    segment_ids,
    tenants,
    adapter_down,
    adapter_up,
):
    sequence_splits = lax.axis_size("uly")
    token_position = queries.shape[1]
    window = token_position * max(1, sequence_splits // 8)
    block_tokens = token_position * sequence_splits
    sub_count = block_tokens // window
    scale = HEAD_SIZE ** (-0.5)
    seg_all = segment_ids[0]
    tenant = tenants[0]
    chosen = jnp.arange(TEN) == tenant
    chosen_f = chosen.astype(jnp.float32)
    down_sel = jnp.sum(
        jnp.where(chosen[:, None, None], adapter_down, jnp.zeros_like(adapter_down)), axis=0
    )
    upward_selected = jnp.sum(
        jnp.where(chosen[:, None, None], adapter_up, jnp.zeros_like(adapter_up)), axis=0
    )
    inputs = layer_input[0]
    columns = inputs
    adapter_lower = jnp.dot(
        columns,
        lax.all_gather(down_sel, ("blk", "uly"), axis=0, tiled=True),
        preferred_element_type=jnp.float32,
    ).astype(jnp.bfloat16)
    head_copies = max(1, sequence_splits // KEY_VALUE_HEADS)
    window_keys = KEY_VALUE_HEADS * head_copies // sequence_splits
    local_heads = QUERY_HEADS // sequence_splits
    group_width = local_heads // window_keys
    query_rows = queries[0].reshape(token_position, QUERY_HEADS, HEAD_SIZE)
    grad_rows = output_gradient[0].reshape(token_position, QUERY_HEADS, HEAD_SIZE)
    key_matrix_rows = jnp.repeat(
        keys[0].reshape(token_position, KEY_VALUE_HEADS, HEAD_SIZE), head_copies, axis=1
    )
    value_matrix_rows = jnp.repeat(
        values[0].reshape(token_position, KEY_VALUE_HEADS, HEAD_SIZE), head_copies, axis=1
    )
    qh, gh, kh, vh = (
        lax.all_to_all(query_rows, "uly", split_axis=1, concat_axis=0, tiled=True),
        lax.all_to_all(grad_rows, "uly", split_axis=1, concat_axis=0, tiled=True),
        lax.all_to_all(key_matrix_rows, "uly", split_axis=1, concat_axis=0, tiled=True),
        lax.all_to_all(value_matrix_rows, "uly", split_axis=1, concat_axis=0, tiled=True),
    )
    q_sub = qh.reshape(sub_count, window, window_keys, group_width, HEAD_SIZE)
    g_sub = gh.reshape(sub_count, window, window_keys, group_width, HEAD_SIZE)
    k_sub = kh.reshape(sub_count, window, window_keys, HEAD_SIZE)
    v_sub = vh.reshape(sub_count, window, window_keys, HEAD_SIZE)
    lse_sub = jnp.transpose(
        saved_log_total[0].reshape(window_keys, group_width, sub_count, window), (2, 0, 1, 3)
    )
    dots_sub = jnp.transpose(
        row_dot_products[0].reshape(window_keys, group_width, sub_count, window), (2, 0, 1, 3)
    )
    block = lax.axis_index("blk")
    start = block * block_tokens
    seg_own = lax.dynamic_slice_in_dim(seg_all, start, block_tokens)
    seg_sub = seg_own.reshape(sub_count, window)
    rows = jnp.arange(window)
    lower = rows[None, :] <= rows[:, None]
    upper = rows[:, None] < rows[None, :]
    tiles_many = jax.vmap(tile_grads, in_axes=(0, 0, 0, 0, 0, 0, 0, None))
    diag_mask = lower[None] & (seg_sub[:, :, None] == seg_sub[:, None, :])
    diag = tiles_many(q_sub, g_sub, lse_sub, dots_sub, k_sub, v_sub, diag_mask, scale)
    back_mask = upper[None] & (seg_sub[1:, :, None] == seg_sub[:-1, None, :])
    back = tiles_many(
        q_sub[1:], g_sub[1:], lse_sub[1:], dots_sub[1:], k_sub[:-1], v_sub[:-1], back_mask, scale
    )
    dq_sub = diag[0] + jnp.concatenate([jnp.zeros_like(back[0][:1]), back[0]], axis=0)
    dk_sub = diag[1] + jnp.concatenate([back[1], jnp.zeros_like(back[1][:1])], axis=0)
    dv_sub = diag[2] + jnp.concatenate([back[2], jnp.zeros_like(back[2][:1])], axis=0)
    k_prev, v_prev = shifted((k_sub[-1], v_sub[-1]), "blk", 1)
    seg_prev = lax.dynamic_slice_in_dim(seg_all, jnp.maximum(start - window, 0), window)
    tile_prev = tile_grads(
        q_sub[0],
        g_sub[0],
        lse_sub[0],
        dots_sub[0],
        k_prev,
        v_prev,
        upper & match(seg_sub[0], seg_prev) & (block > 0),
        scale,
    )
    key_back, value_back = shifted((tile_prev[1], tile_prev[2]), "blk", -1)
    dq_sub = dq_sub.at[0].add(tile_prev[0])
    dk_sub = dk_sub.at[-1].add(key_back)
    dv_sub = dv_sub.at[-1].add(value_back)
    query_gradient = dq_sub.astype(jnp.bfloat16).reshape(block_tokens, local_heads * HEAD_SIZE)
    key_heads = dk_sub.reshape(block_tokens, window_keys, HEAD_SIZE)
    value_heads = dv_sub.reshape(block_tokens, window_keys, HEAD_SIZE)
    key_token_rows, value_token_rows = (
        lax.all_to_all(
            key_heads.astype(jnp.bfloat16), "uly", split_axis=0, concat_axis=1, tiled=True
        ).astype(key_heads.dtype),
        lax.all_to_all(
            value_heads.astype(jnp.bfloat16), "uly", split_axis=0, concat_axis=1, tiled=True
        ).astype(value_heads.dtype),
    )
    key_grad = (
        key_token_rows.reshape(token_position, KEY_VALUE_HEADS, head_copies, HEAD_SIZE)
        .sum(axis=2)
        .astype(jnp.bfloat16)
        .reshape(1, token_position, KEY_VALUE_HEADS * HEAD_SIZE)
    )
    value_grad = (
        value_token_rows.reshape(token_position, KEY_VALUE_HEADS, head_copies, HEAD_SIZE)
        .sum(axis=2)
        .astype(jnp.bfloat16)
        .reshape(1, token_position, KEY_VALUE_HEADS * HEAD_SIZE)
    )
    lower_block = lax.all_gather(adapter_lower, "uly", axis=0, tiled=True)
    dq_tokens = lax.all_to_all(
        query_gradient.reshape(block_tokens, local_heads, HEAD_SIZE),
        "uly",
        split_axis=0,
        concat_axis=1,
        tiled=True,
    )
    up_full = lax.all_gather(upward_selected, "uly", axis=1, tiled=True)
    coefficient = jnp.dot(
        dq_tokens.reshape(token_position, QUERY_HEADS * HEAD_SIZE),
        up_full.T,
        preferred_element_type=jnp.float32,
    )
    upward_partial = ADAPTER_SCALE * jnp.dot(
        lower_block.T, query_gradient, preferred_element_type=jnp.float32
    )
    coefficient_lower = (ADAPTER_SCALE * coefficient).astype(jnp.bfloat16)
    columns = inputs
    down_part = lax.psum_scatter(
        jnp.dot(columns.T, coefficient_lower, preferred_element_type=jnp.float32),
        ("blk", "uly"),
        scatter_dimension=0,
        tiled=True,
    )
    down_grad = lax.psum(chosen_f[:, None, None] * down_part[None], "dp")
    up_grad = lax.psum(chosen_f[:, None, None] * upward_partial[None], ("dp", "blk"))
    return (key_grad, value_grad, down_grad, up_grad)


def solution(mesh):
    placed = (
        P("dp", ("blk", "uly"), None),
        P("dp", ("blk", "uly"), None),
        P("dp", ("blk", "uly"), None),
        P("dp", ("blk", "uly"), None),
        P("dp", ("blk", "uly"), None),
        P("dp", "uly", "blk"),
        P("dp", "uly", "blk"),
        P("dp", None),
        P("dp"),
        P(None, ("blk", "uly"), None),
        P(None, None, "uly"),
    )
    return jax.shard_map(
        local,
        mesh=mesh,
        in_specs=placed,
        out_specs=(
            P("dp", ("blk", "uly"), None),
            P("dp", ("blk", "uly"), None),
            P(None, ("blk", "uly"), None),
            P(None, None, "uly"),
        ),
        check_vma=False,
    )
```

profile of v0, /device:TPU:4, one launch (start us, length us, event | category | flops | bytes accessed | tf_op | source)
XLA Modules:
  0.0 1200.4 jit_solution(14515156804777337000)
XLA Ops:
  8.0 1.1 reshape_squeeze.18
  9.9 15.1 %all-to-all-start = ((bf16[128,8,128]{2,0,1:T(8,128)(2,1)}), bf16[128,8,128]{2,0,1:T(8,128)(2,1)S(1)}, u32[]{:S(2)}, u32[]{:S(2)}) async-start(bf16[128,8,128]{2,0,1:T(8,128)(2,1)} %bitcast.1), calls=%async_computation | async-start | bytes 524288 | tf_op jit(solution)/shard_map/all_to_all | solution.py:89
  25.9 18.2 %all-to-all-done = bf16[128,8,128]{2,0,1:T(8,128)(2,1)S(1)} async-done(((bf16[128,8,128]{2,0,1:T(8,128)(2,1)}), bf16[128,8,128]{2,0,1:T(8,128)(2,1)S(1)}, u32[]{:S(2)}, u32[]{:S(2)}) %all-to-all-start) | async-done | bytes 262176 | tf_op jit(solution)/shard_map/all_to_all | solution.py:89
  44.9 5.9 all-to-all-start.2
  50.7 1.4 copy.86
  52.2 1.4 copy.51
  53.6 16.3 %all-to-all-done.2 = bf16[128,8,128]{2,0,1:T(8,128)(2,1)S(1)} async-done(((bf16[128,8,128]{2,0,1:T(8,128)(2,1)}), bf16[128,8,128]{2,0,1:T(8,128)(2,1)S(1)}, u32[]{:S(2)}, u32[]{:S(2)}) %all-to-all-start.2) | async-done | bytes 262176 | tf_op jit(solution)/shard_map/all_to_all | solution.py:90
  70.5 5.7 all-to-all-start.1
  76.2 1.4 copy.87
  77.7 1.4 copy.54
  79.1 53.0 %all-to-all-done.1 = bf16[128,32,128]{2,0,1:T(8,128)(2,1)S(1)} async-done(((bf16[128,32,128]{2,0,1:T(8,128)(2,1)}), bf16[128,32,128]{2,0,1:T(8,128)(2,1)S(1)}, u32[]{:S(2)}, u32[]{:S(2)}) %all-to-all-start.1) | async-done | bytes 1048608 | tf_op jit(solution)/shard_map/all_to_all | solution.py:87
  132.1 1.0 copy-done.3
  133.1 3.6 all-to-all-start.3
  142.5 3.1 collective-permute-start
  145.6 1.4 slice_bitcast_fusion.11
  147.0 1.9 collective-permute-start.1
  148.9 2.9 fusion.10
  151.9 40.2 %all-to-all-done.3 = bf16[128,32,128]{2,0,1:T(8,128)(2,1)S(1)} async-done(((bf16[128,32,128]{2,0,1:T(8,128)(2,1)}), bf16[128,32,128]{2,0,1:T(8,128)(2,1)S(1)}, u32[]{:S(2)}, u32[]{:S(2)}) %all-to-all-start.3) | async-done | bytes 1048608 | tf_op jit(solution)/shard_map/all_to_all | solution.py:88
  192.1 1.9 fusion.12
  194.5 1.0 copy-done.4
  202.7 1.8 copy.64
  204.5 4.2 all-to-all-start.6
  210.4 61.0 %all_gather.9 = bf16[16,4096]{1,0:T(8,128)(2,1)} all-gather(bf16[16,512]{1,0:T(8,128)(2,1)S(1)} %select_reduce_fusion), channel_id=1, replica_groups=mesh['dp'=4,'blk'=16,'uly'=8] {'uly'}, dimensions={1}, use_global_device_ids=true | all-gather | bytes 147456 | tf_op jit(solution)/shard_map/all_gather | solution.py:166
  272.4 2.5 collective-permute-start.3
  274.9 1.9 convolution_bitcast_fusion.3
  278.3 1.2 fusion.18
  280.0 1.5 reduce.15
  281.5 1.7 reshape.424
  283.2 6.6 all-to-all-start.5
  290.8 2.4 collective-permute-start.2
  293.2 2.6 fusion.16
  295.7 1.4 copy.65
  297.1 1.3 copy.66
  298.4 1.8 convolution_bitcast_fusion
  300.3 2.7 copy.82
  303.0 1.0 copy-done.12
  306.5 2.0 all-to-all-done.5
  308.5 10.0 all-to-all-start.4
  318.5 199.6 %all-gather = bf16[128,64,16]{1,2,0:T(8,128)(2,1)S(1)} all-gather(bf16[1,64,16]{1,2,0:T(8,128)(2,1)S(1)} %bitcast.367), channel_id=1, replica_groups=mesh['dp'=4,'blk'=16,'uly'=8] {'blk','uly'}, dimensions={0}, use_global_device_ids=true | all-gather | bytes 264192 | tf_op jit(solution)/shard_map/all_gather | solution.py:71
  519.0 1.5 reshape.405
  521.2 20.2 %all_gather.11 = bf16[1024,16]{0,1:T(8,128)(2,1)S(1)} all-gather(bf16[128,16]{0,1:T(8,128)(2,1)S(1)} %fusion.36), channel_id=1, replica_groups=mesh['dp'=4,'blk'=16,'uly'=8] {'uly'}, dimensions={0}, use_global_device_ids=true | all-gather | bytes 36864 | tf_op jit(solution)/shard_map/all_gather | solution.py:158
  541.4 1.5 copy.68
  542.8 1.6 convolution_multiply_fusion.2
  546.5 1.2 reshape.423
  548.7 458.1 %reduce-scatter.4.cloned.1.call-done = f32[64,16]{1,0:T(8,128)} async-done(((f32[8192,16]{1,0:T(8,128)}), f32[64,16]{1,0:T(8,128)}) %reduce-scatter.4.cloned.1.call-update) | async-done | bytes 4112
  1007.7 17.6 %psum.14 = f32[4,64,16]{1,2,0:T(8,128)} all-reduce(f32[4,64,16]{1,2,0:T(8,128)S(1)} %broadcast_multiply_fusion.1), channel_id=1, replica_groups=mesh['dp'=4,'blk'=16,'uly'=8] {'dp'}, use_global_device_ids=true, to_apply=%region_4.5 | all-reduce | flops 4096 | bytes 32768 | tf_op jit(solution)/shard_map/psum | solution.py:183
  1025.3 166.1 %all-reduce.5.cloned.1.call-done = f32[4,16,512]{2,1,0:T(8,128)} async-done(((f32[4,16,512]{2,1,0:T(8,128)}), f32[4,16,512]{2,1,0:T(8,128)}) %all-reduce.5.cloned.1.call-update) | async-done | bytes 131088 | tf_op jit(solution)/shard_map/psum | solution.py:184
  1191.4 1.6 copy.100
  (110 shorter events, 29.3 us)
Async XLA Ops:
  8.0 290.4 %copy-start = (bf16[1,128,8192]{2,1,0:T(8,128)(2,1)S(1)}, bf16[1,128,8192]{2,1,0:T(8,128)(2,1)}, u32[]{:S(2)}) copy-start(bf16[1,128,8192]{2,1,0:T(8,128)(2,1)} %param.21) | copy-start | bytes 6291460
  9.9 34.3 %all-to-all-start = ((bf16[128,8,128]{2,0,1:T(8,128)(2,1)}), bf16[128,8,128]{2,0,1:T(8,128)(2,1)S(1)}, u32[]{:S(2)}, u32[]{:S(2)}) async-start(bf16[128,8,128]{2,0,1:T(8,128)(2,1)} %bitcast.1), calls=%async_computation | async-start | bytes 524288 | tf_op jit(solution)/shard_map/all_to_all | solution.py:89
  44.9 25.0 %all-to-all-start.2 = ((bf16[128,8,128]{2,0,1:T(8,128)(2,1)}), bf16[128,8,128]{2,0,1:T(8,128)(2,1)S(1)}, u32[]{:S(2)}, u32[]{:S(2)}) async-start(bf16[128,8,128]{2,0,1:T(8,128)(2,1)} %bitcast.14), calls=%async_computation.2 | async-start | bytes 524288 | tf_op jit(solution)/shard_map/all_to_all | solution.py:90
  69.8 0.7 copy-start.13
  70.5 61.5 %all-to-all-start.1 = ((bf16[128,32,128]{2,0,1:T(8,128)(2,1)}), bf16[128,32,128]{2,0,1:T(8,128)(2,1)S(1)}, u32[]{:S(2)}, u32[]{:S(2)}) async-start(bf16[128,32,128]{2,0,1:T(8,128)(2,1)} %copy.51), calls=%async_computation.1 | async-start | bytes 2097152 | tf_op jit(solution)/shard_map/all_to_all | solution.py:87
  77.7 61.3 %copy-start.18 = (f32[1,4,1024]{2,1,0:T(4,128)S(1)}, f32[1,4,1024]{2,1,0:T(4,128)}, u32[]{:S(2)}) copy-start(f32[1,4,1024]{2,1,0:T(4,128)} %param.22) | copy-start | bytes 49156
  77.7 61.9 %copy-start.19 = (f32[1,4,1024]{2,1,0:T(4,128)S(1)}, f32[1,4,1024]{2,1,0:T(4,128)}, u32[]{:S(2)}) copy-start(f32[1,4,1024]{2,1,0:T(4,128)} %param.23) | copy-start | bytes 49156
  132.1 1.0 copy-start.3
  133.1 59.0 %all-to-all-start.3 = ((bf16[128,32,128]{2,0,1:T(8,128)(2,1)}), bf16[128,32,128]{2,0,1:T(8,128)(2,1)S(1)}, u32[]{:S(2)}, u32[]{:S(2)}) async-start(bf16[128,32,128]{2,0,1:T(8,128)(2,1)} %copy.54), calls=%async_computation.3 | async-start | bytes 2097152 | tf_op jit(solution)/shard_map/all_to_all | solution.py:88
  142.5 56.0 %collective-permute-start = (bf16[128,1,128]{2,0,1:T(8,128)(2,1)}, bf16[128,1,128]{2,0,1:T(8,128)(2,1)}, u32[]{:S(2)}, u32[]{:S(2)}) collective-permute-start(bf16[128,1,128]{2,0,1:T(8,128)(2,1)} %slice_bitcast_fusion.12), channel_id=1, source_target_pairs={{0,8},{8,16},{16,24},{24,32},{32,40},{40,48},{48,56},{56,64},{64,7... | collective-permute-start | bytes 98312 | tf_op jit(solution)/shard_map/ppermute | solution.py:18
  147.0 52.4 %collective-permute-start.1 = (bf16[128,1,128]{2,0,1:T(8,128)(2,1)}, bf16[128,1,128]{2,0,1:T(8,128)(2,1)}, u32[]{:S(2)}, u32[]{:S(2)}) collective-permute-start(bf16[128,1,128]{2,0,1:T(8,128)(2,1)} %slice_bitcast_fusion.11), channel_id=1, source_target_pairs={{0,8},{8,16},{16,24},{24,32},{32,40},{40,48},{48,56},{56,64},{64,7... | collective-permute-start | bytes 98312 | tf_op jit(solution)/shard_map/ppermute | solution.py:18
  194.0 2.1 copy-start.10
  194.0 1.6 copy-start.4
  194.5 1.6 copy-start.14
  194.5 1.6 copy-start.20
  196.1 1.4 copy-start.1
  197.5 1.0 copy-start.7
  197.5 1.0 copy-start.21
  197.5 1.0 copy-start.23
  197.5 2.0 copy-start.22
  201.6 1.0 copy-start.8
  204.5 78.8 %all-to-all-start.6 = ((bf16[1024,4,128]{2,1,0:T(4,128)(2,1)}), bf16[1024,4,128]{2,1,0:T(4,128)(2,1)}, u32[]{:S(2)}, u32[]{:S(2)}) async-start(bf16[1024,4,128]{2,1,0:T(4,128)(2,1)} %copy.64), calls=%async_computation.6 | async-start | bytes 2097152 | tf_op jit(solution)/shard_map/all_to_all | solution.py:159
  208.7 68.1 %copy-start.2 = (f32[8,1,4,128,128]{3,4,2,0,1:T(8,128)S(1)}, f32[8,1,4,128,128]{3,4,2,0,1:T(8,128)}, u32[]{:S(2)}) copy-start(f32[8,1,4,128,128]{3,4,2,0,1:T(8,128)} %copy-done.1) | copy-start | bytes 6291460
  272.4 7.1 collective-permute-start.3
  276.8 1.2 copy-start.5
  276.8 1.5 copy-start.11
  278.3 11.7 copy-start.6
  283.2 25.2 %all-to-all-start.5 = ((bf16[8,2,8192]{2,1,0:T(2,128)(2,1)}), bf16[8,2,8192]{2,1,0:T(2,128)(2,1)S(1)}, u32[]{:S(2)}, u32[]{:S(2)}) async-start(bf16[8,2,8192]{2,1,0:T(2,128)(2,1)} %reshape.424), calls=%async_computation.5 | async-start | bytes 524288 | tf_op jit(solution)/shard_map/all_to_all | solution.py:142
  289.9 716.9 %reduce-scatter.4.cloned.1.call-start = ((), (), s32[]{:S(2)}) async-start(), calls=%async_computation.9 | async-start | bytes 4227072
  290.8 12.2 %collective-permute-start.2 = (f32[128,1,128]{2,0,1:T(8,128)}, f32[128,1,128]{2,0,1:T(8,128)}, u32[]{:S(2)}, u32[]{:S(2)}) collective-permute-start(f32[128,1,128]{2,0,1:T(8,128)} %fusion.31), channel_id=1, source_target_pairs={{8,0},{16,8},{24,16},{32,24},{40,32},{48,40},{56,48},{64,56},{72,6... | collective-permute-start | bytes 196616 | tf_op jit(solution)/shard_map/ppermute | solution.py:18
  295.7 2.7 copy-start.17
  302.9 1.0 copy-start.12
  308.5 209.6 %copy-start.15 = (bf16[8,2,8192]{2,1,0:T(2,128)(2,1)}, bf16[8,2,8192]{2,1,0:T(2,128)(2,1)S(1)}, u32[]{:S(2)}) copy-start(bf16[8,2,8192]{2,1,0:T(2,128)(2,1)S(1)} %all-to-all-done.5) | copy-start | bytes 786436
  308.5 238.1 %all-to-all-start.4 = ((bf16[8,2,8192]{2,1,0:T(2,128)(2,1)}), bf16[8,2,8192]{2,1,0:T(2,128)(2,1)}, u32[]{:S(2)}, u32[]{:S(2)}) async-start(bf16[8,2,8192]{2,1,0:T(2,128)(2,1)} %reshape.422), calls=%async_computation.4 | async-start | bytes 524288 | tf_op jit(solution)/shard_map/all_to_all | solution.py:139
  318.5 872.9 %all-reduce.5.cloned.1.call-start = ((), (), s32[]{:S(2)}) async-start(), calls=%async_computation.8 | async-start | bytes 262144 | tf_op jit(solution)/shard_map/psum | solution.py:184
  518.1 23.3 %copy-start.9 = (bf16[8,128,1,4,128]{4,1,3,0,2:T(8,128)(2,1)S(1)}, bf16[8,128,1,4,128]{4,1,3,0,2:T(8,128)(2,1)}, u32[]{:S(2)}) copy-start(bf16[8,128,1,4,128]{4,1,3,0,2:T(8,128)(2,1)} %copy-done.8) | copy-start | bytes 3145732
  521.2 24.1 %copy-start.16 = (bf16[8,2,8192]{2,1,0:T(2,128)(2,1)S(1)}, bf16[8,2,8192]{2,1,0:T(2,128)(2,1)}, u32[]{:S(2)}) copy-start(bf16[8,2,8192]{2,1,0:T(2,128)(2,1)} %copy-done.15) | copy-start | bytes 786436
Sparse Core Ops, SparseCore 0:
  303.1 703.6 reduce-scatter.3
Sparse Core Ops, SparseCore 1:
  545.3 646.0 all-reduce.4
where the time goes:
time: 1200 us
  waiting for transfers between devices  754 us (63%)
  blocking collectives  298 us (25%)
  starting transfers between devices  61.1 us (5%)
  local copies, waits for them, and re-layouts  42.2 us (4%)
  matrix products  20.9 us (2%)
  between operations  16.8 us (1%)
    unnamed x3, waiting for transfers between devices  458 us
    all_gather x1, blocking collectives, local(): lax.all_gather(down_sel, ('blk', 'uly'), axis=0, tiled=True)  200 us
    psum x1, waiting for transfers between devices, local(): lax.psum(chosen_f[:, None, None] * upward_partial[None], ('dp', 'blk'))  166 us
    all_gather x1, blocking collectives, local(): up_full = lax.all_gather(upward_selected, 'uly', axis=1, tiled=True)  61 us
    all_to_all x1, waiting for transfers between devices, local(): lax.all_to_all(query_rows, 'uly', split_axis=1, concat_axis=0, tiled=True)  53 us
    all_to_all x1, waiting for transfers between devices, local(): lax.all_to_all(grad_rows, 'uly', split_axis=1, concat_axis=0, tiled=True)  40.2 us
  transfers between devices with their start and end apart: 13, of which 7 were waited for; matrix products, arithmetic and copies ran while one was open for 5% of the time, Pallas kernels for 0%

commit v1 on v0

v1 whole, which is shorter than its diff:
```python
import jax
import jax.numpy as jnp
from jax import lax
from jax.experimental import pallas as pl
from jax.experimental.pallas import tpu as pltpu
from jax.sharding import PartitionSpec as P

MESH = pl.DeviceIdType.MESH
F32 = jnp.float32
BF16 = jnp.bfloat16

HEAD = 128
HEADS = 32
KV = 4
GROUP = HEADS // KV
TEN = 4
R = 16
TOK = 128
D = 8192
SEQ = 16384
WIDE = HEADS * HEAD
SCALE = HEAD ** -0.5
LOG2E = 1.4426950408889634
ADAPTER_SCALE = 2.0
NT = (((1,), (1,)), ((), ()))
NN = (((1,), (0,)), ((), ()))
TN = (((0,), (0,)), ((), ()))


def dot(a, b, dims):
    return lax.dot_general(a, b, dims, preferred_element_type=F32)


def mod(a, n):
    return lax.rem(a, jnp.int32(n))


def div(a, n):
    return lax.div(a, jnp.int32(n))


class Sems:
    def __init__(self):
        self.count = 0

    def take(self, n):
        first = self.count
        self.count += n
        return first


def layout():
    s = Sems()
    names = dict(
        ld=7, kv=4, dkv=4, au=7, ten=3, a2=15, u3=3, cu=1, cd=1, xu=3, xd=3,
        zhu=3, zhd=3, zlu=3, zld=3, xyu=15, xyd=3,
    )
    return {name: s.take(n) for name, n in names.items()}, s.count


SEM, N_SEM = layout()
L_KV, L_LD, L_SEG, L_ADN, L_AUP, L_Q, L_G, L_X, L_OUT, N_LOC = 0, 8, 10, 12, 13, 14, 15, 16, 17, 21


def kernel(
    ten_s, q_h, k_h, v_h, g_h, x_h, lse_h, dots_h, seg_h, adn_h, aup_h,
    kg_o, vg_o, down_o, up_o,
    q_v, g_v, x_v, kv_v, halo, ld_v, ld_all, seg_v, adn_v, aup_v, bias_v,
    dkv_own, dkv_out, dkv_in, dqt, au, ag, ug, ten_v,
    s1u, s1d, rcu, rcd, s2u, s2d, rxu, rxd, s3u, s3d, rhu, rhd, s4u, s4d, rlu, rld, fu, fd, kg_v, vg_v, down_v, up_v,
    loc, ssem, rsem,
):
    y = lax.axis_index("dp")
    b = lax.axis_index("blk")
    u = lax.axis_index("uly")
    zl, x = div(b, 4), mod(b, 4)
    zh, c = div(u, 2), mod(u, 2)
    t = b * 8 + u

    def dev(y_=y, zl_=zl, x_=x, zh_=zh, c_=c):
        return (y_, zl_ * 4 + x_, zh_ * 2 + c_)

    def token_dev(t_):
        return (y, div(t_, 8), mod(t_, 8))

    following = token_dev(mod(t + 1, 128))
    previous = token_dev(mod(t + 127, 128))

    def local(src, dst, i):
        return pltpu.make_async_copy(src, dst, loc.at[i])

    def remote(src, dst, i, to):
        return pltpu.make_async_remote_copy(
            src_ref=src, dst_ref=dst, send_sem=ssem.at[i], recv_sem=rsem.at[i], device_id=to, device_id_type=MESH
        )

    peers = [previous, following]
    peers += [dev(zh_=mod(zh + k, 4)) for k in (1, 2, 3)]
    peers += [dev(zh_=mod(zh + k, 4), c_=1 - c) for k in (0, 1, 2, 3)]
    plane = [(i, j) for i in range(4) for j in range(4) if (i, j) != (0, 0)]
    peers += [dev(zl_=mod(zl + i, 4), x_=mod(x + j, 4)) for i, j in plane]
    peers += [dev(y_=mod(y + i, 4), x_=mod(x + j, 4)) for i, j in plane if i != 0]
    barrier = pltpu.get_barrier_semaphore()
    for to in peers:
        pl.semaphore_signal(barrier, inc=1, device_id=to, device_id_type=MESH)

    small = [
        local(adn_h, adn_v, L_ADN),
        local(aup_h, aup_v, L_AUP),
        local(lse_h.at[0], ld_v.at[0], L_LD),
        local(dots_h.at[0], ld_v.at[1], L_LD + 1),
        local(seg_h.at[:, pl.ds(pl.multiple_of(t * TOK, TOK), TOK)], seg_v.at[1], L_SEG),
        local(seg_h.at[:, pl.ds(pl.multiple_of(mod(t + 127, 128) * TOK, TOK), TOK)], seg_v.at[0], L_SEG + 1),
    ]
    kv_loads = []
    for i in range(KV):
        kv_loads.append(local(k_h.at[0, :, pl.ds(i * HEAD, HEAD)], kv_v.at[i, 0], L_KV + 2 * i))
        kv_loads.append(local(v_h.at[0, :, pl.ds(i * HEAD, HEAD)], kv_v.at[i, 1], L_KV + 2 * i + 1))
    big = [local(q_h.at[0], q_v, L_Q), local(g_h.at[0], g_v, L_G)]
    x_load = local(x_h.at[0], x_v, L_X)
    for copy in small + kv_loads + big + [x_load]:
        copy.start()

    for copy in small:
        copy.wait()
    tenant = jnp.full((R, 128), ten_s[0], jnp.int32)
    ten_v[y] = tenant.astype(F32).astype(BF16)
    down_sel = jnp.zeros((R, 64), F32)
    up_sel = jnp.zeros((R, 128), F32)
    for a in range(TEN):
        down_sel += jnp.where(tenant[:, :64] == a, adn_v[a].astype(F32), 0.0)
        up_sel += jnp.where(tenant == a, aup_v[a, :, pl.ds(pl.multiple_of(x * 128, 128), 128)].astype(F32), 0.0)
    place = lax.broadcasted_iota(jnp.int32, (64, 128), 1) - lax.broadcasted_iota(jnp.int32, (64, 128), 0)
    shift = jnp.where(place == c * 64, 1.0, 0.0).astype(BF16)
    au[u, 0] = dot(down_sel.astype(BF16), shift, NN).astype(BF16)
    au[u, 1] = up_sel.astype(BF16)
    ld_all[u] = ld_v[:, :, pl.ds(pl.multiple_of(u * TOK, TOK), TOK)]
    row = lax.broadcasted_iota(jnp.int32, (TOK, TOK), 0)
    col = lax.broadcasted_iota(jnp.int32, (TOK, TOK), 1)
    ids_now = jnp.broadcast_to(seg_v[1].astype(F32), (TOK, TOK))
    ids_before = jnp.broadcast_to(seg_v[0].astype(F32), (TOK, TOK))
    now_rows = jnp.sum(jnp.where(row == col, ids_now, 0.0), axis=1, keepdims=True)
    before_rows = jnp.sum(jnp.where(row == col, ids_before, 0.0), axis=1, keepdims=True)
    first = jnp.broadcast_to(t, (TOK, TOK)) > 0
    bias_v[:TOK] = jnp.where((row > col) & (before_rows == ids_now) & first, 0.0, -1e30)
    bias_v[TOK:] = jnp.where((row <= col) & (now_rows == ids_now), 0.0, -1e30)

    for copy in kv_loads:
        copy.wait()
    pl.semaphore_wait(barrier, len(peers))

    sent = []

    def go(copy):
        copy.start()
        sent.append(copy)
        return copy

    other_core = dev(c_=1 - c)
    au_copies, ld_copies = [], []
    others = [(k, other) for k in (2, 1, 3, 0) for other in (0, 1) if (k, other) != (0, 0)]
    for n, (k, other) in enumerate(others):
        to = dev(zh_=mod(zh + k, 4), c_=(1 - c) if other else c)
        au_copies.append(go(remote(au.at[u], au.at[u], SEM["au"] + n, to)))
    for n, (k, other) in enumerate(others):
        zh_to = mod(zh + k, 4)
        c_to = (1 - c) if other else c
        piece = pl.ds(pl.multiple_of((zh_to * 2 + c_to) * TOK, TOK), TOK)
        ld_copies.append(go(remote(ld_v.at[:, :, piece], ld_all.at[u], SEM["ld"] + n, dev(zh_=zh_to, c_=c_to))))
    kv_copies = [go(remote(kv_v.at[i], halo.at[i], SEM["kv"] + i, following)) for i in range(KV)]
    tens = [
        go(remote(ten_v.at[y], ten_v.at[y], SEM["ten"] + k - 1, dev(y_=mod(y + k, 4)))) for k in (1, 2, 3)
    ]

    for copy in au_copies:
        copy.wait_recv()
    for j in range(4):
        ag[zl, x, j] = au[2 * j, 0] + au[2 * j + 1, 0]
    for j in range(8):
        ug[x, j] = au[j, 1]
    a2 = []
    for n, (i, j) in enumerate(plane):
        to = dev(zl_=mod(zl + i, 4), x_=mod(x + j, 4))
        a2.append(go(remote(ag.at[zl, x], ag.at[zl, x], SEM["a2"] + n, to)))
    u3 = [go(remote(ug.at[x], ug.at[x], SEM["u3"] + k - 1, dev(x_=mod(x + k, 4)))) for k in (1, 2, 3)]
    for copy in big:
        copy.wait()
    for copy in ld_copies:
        copy.wait_recv()

    def one_head(i):
        keys = jnp.concatenate([halo[i, 0], kv_v[i, 0]], axis=0)
        values = jnp.concatenate([halo[i, 1], kv_v[i, 1]], axis=0)
        q_list, g_list, p_list, s_list = [], [], [], []
        for half in range(2):
            heads = range(half * 4, half * 4 + 4)
            q = jnp.concatenate([q_v[:, (i * GROUP + h) * HEAD:(i * GROUP + h + 1) * HEAD] for h in heads], axis=0)
            g = jnp.concatenate([g_v[:, (i * GROUP + h) * HEAD:(i * GROUP + h + 1) * HEAD] for h in heads], axis=0)
            scores = dot(keys, q, NT)
            grads = dot(values, g, NT)
            q_list.append(q)
            g_list.append(g)
            for n in range(4):
                at = slice(n * TOK, (n + 1) * TOK)
                lse = ld_all[2 * i + half, 0, n:n + 1] * LOG2E
                dots = ld_all[2 * i + half, 1, n:n + 1]
                probs = jnp.exp2((scores[:, at] * (SCALE * LOG2E) - lse) + bias_v[...])
                p_list.append(probs.astype(BF16))
                s_list.append((probs * (grads[:, at] - dots)).astype(BF16))
        score_grad = jnp.concatenate(s_list, axis=1)
        value_part = dot(jnp.concatenate(p_list, axis=1), jnp.concatenate(g_list, axis=0), NN)
        key_part = dot(score_grad, jnp.concatenate(q_list, axis=0), NN) * SCALE
        query_part = (dot(keys, score_grad, TN) * SCALE).astype(BF16)
        dkv_out[i, 0] = key_part[:TOK].astype(BF16)
        dkv_out[i, 1] = value_part[:TOK].astype(BF16)
        dkv_own[i, 0] = key_part[TOK:]
        dkv_own[i, 1] = value_part[TOK:]
        for h in range(GROUP):
            dqt[(i * GROUP + h) * HEAD:(i * GROUP + h + 1) * HEAD] = query_part[:, h * HEAD:(h + 1) * HEAD]

    dkv_copies = [remote(dkv_out.at[i], dkv_in.at[i], SEM["dkv"] + i, previous) for i in range(KV)]

    for i in range(KV):
        kv_copies[i].wait_recv()
        one_head(i)
        go(dkv_copies[i])

    for copy in u3:
        copy.wait_recv()
    x_load.wait()

    def to_three(name, source, target, place, axis):
        copies = []
        for k in (2, 1, 3):
            to = mod(place + k, 4)
            copies.append(go(remote(source(to), target.at[k - 1], SEM[name] + k - 1, dev(**{axis: to}))))
        return copies

    def sum_of_four(own, target, copies):
        total = own.astype(F32)
        for k, copy in zip((2, 1, 3), copies):
            copy.wait_recv()
            total += target[k - 1].astype(F32)
        return total.astype(BF16)

    up_rows = jnp.concatenate([ug[k, n] for n in range(8) for k in range(4)], axis=1)
    coeff = (ADAPTER_SCALE * dot(up_rows, dqt[...], NN)).astype(BF16)
    left = lax.broadcasted_iota(jnp.int32, (R, 128), 1) < 64
    for m in range(2):
        part = dot(coeff, x_v[:, m * 4096:(m + 1) * 4096], NN)
        for n in range(4):
            for j in range(4):
                a = part[:, (n * 4 + j) * 128:(n * 4 + j + 1) * 128]
                d = part[:, 2048 + (n * 4 + j) * 128:2048 + (n * 4 + j + 1) * 128]
                s1d[0, n, j, m] = jnp.where(left, a, pltpu.roll(d, 64, 1)).astype(BF16)
                s1d[1, n, j, m] = jnp.where(left, pltpu.roll(a, 64, 1), d).astype(BF16)
    cd = go(remote(s1d.at[1 - c], rcd, SEM["cd"], other_core))

    cd.wait_recv()
    s2d[...] = (s1d[c].astype(F32) + rcd[...].astype(F32)).astype(BF16)
    xd = to_three("xd", lambda to: s2d.at[to], rxd, x, "x_")

    for copy in a2:
        copy.wait_recv()
    down_rows = jnp.concatenate([ag[i, j, k] for i in range(4) for j in range(4) for k in range(4)], axis=1)
    low = (ADAPTER_SCALE * dot(down_rows, x_v[...], NT).astype(BF16).astype(F32)).astype(BF16)
    for n in range(KV):
        part = dot(low, dqt[n * 1024:(n + 1) * 1024], NT)
        for j in range(2):
            for k in range(4):
                s1u[j, k, n] = part[:, (j * 4 + k) * 128:(j * 4 + k + 1) * 128].astype(BF16)
    cu = go(remote(s1u.at[1 - c], rcu, SEM["cu"], other_core))
    s3d[...] = sum_of_four(s2d[x], rxd, xd)
    zhd = to_three("zhd", lambda to: s3d.at[to], rhd, zh, "zh_")
    cu.wait_recv()
    s2u[...] = (s1u[c].astype(F32) + rcu[...].astype(F32)).astype(BF16)
    xu = to_three("xu", lambda to: s2u.at[to], rxu, x, "x_")
    s3u[...] = sum_of_four(s2u[x], rxu, xu)
    zhu = to_three("zhu", lambda to: s3u.at[to], rhu, zh, "zh_")
    s4d[...] = sum_of_four(s3d[zh], rhd, zhd)
    zld = to_three("zld", lambda to: s4d.at[div(to, 2)], rld, zl, "zl_")
    s4u[...] = sum_of_four(s3u[zh], rhu, zhu)
    zlu = to_three("zlu", lambda to: s4u, rlu, zl, "zl_")

    early = list(sent)
    last = []
    fd[y] = sum_of_four(s4d[div(zl, 2)], rld, zld)
    for k in (2, 1, 3):
        last.append(remote(fd.at[y], fd.at[y], SEM["xyd"] + k - 1, dev(y_=mod(y + k, 4))))
        last[-1].start()
    fu[y, x] = sum_of_four(s4u[...], rlu, zlu)
    for n, (i, j) in enumerate(plane):
        to = dev(y_=mod(y + i, 4), x_=mod(x + j, 4))
        last.append(remote(fu.at[y, x], fu.at[y, x], SEM["xyu"] + n, to))
        last[-1].start()

    for copy in early:
        copy.wait_send()
    for i in range(KV):
        dkv_copies[i].wait_recv()
        at = slice(i * HEAD, (i + 1) * HEAD)
        kg_v[0, :, at] = (dkv_own[i, 0] + dkv_in[i, 0].astype(F32)).astype(BF16)
        vg_v[0, :, at] = (dkv_own[i, 1] + dkv_in[i, 1].astype(F32)).astype(BF16)
    results = [local(kg_v, kg_o, L_OUT), local(vg_v, vg_o, L_OUT + 1)]
    for copy in results:
        copy.start()

    for copy in last + tens:
        copy.wait_recv()
    odd = jnp.broadcast_to(mod(zl, 2), (R, 64)) > 0
    for a in range(TEN):
        down = jnp.zeros((R, 128), F32)
        for j in range(4):
            down += jnp.where(ten_v[j].astype(F32) == a, fd[j].astype(F32), 0.0)
        down_v[a] = jnp.where(odd, down[:, 64:], down[:, :64])
        for k in range(4):
            up = jnp.zeros((R, 128), F32)
            for j in range(4):
                up += jnp.where(ten_v[j].astype(F32) == a, fu[j, k].astype(F32), 0.0)
            up_v[a, :, k * 128:(k + 1) * 128] = up

    results += [local(down_v, down_o, L_OUT + 2), local(up_v, up_o, L_OUT + 3)]
    for copy in results[2:]:
        copy.start()
    for copy in last:
        copy.wait_send()
    for copy in results:
        copy.wait()


def hand_over(*refs):
    given, taken, held, sems = refs[:4], refs[4:8], refs[8:12], refs[12]
    inward = [pltpu.make_async_copy(given[i], held[i], sems.at[0, i]) for i in range(4)]
    outward = [pltpu.make_async_copy(held[i], taken[i], sems.at[1, i]) for i in range(4)]
    for copy in inward:
        copy.start()
    for before, after in zip(inward, outward):
        before.wait()
        after.start()
    for copy in outward:
        copy.wait()


def local(queries, keys, values, output_gradient, layer_input, saved_log_total, row_dot_products, segment_ids, tenants,
          adapter_down, adapter_up):
    anywhere = pl.BlockSpec(memory_space=pl.ANY)
    results = (
        jax.ShapeDtypeStruct((1, TOK, KV * HEAD), BF16),
        jax.ShapeDtypeStruct((1, TOK, KV * HEAD), BF16),
        jax.ShapeDtypeStruct((TEN, R, 64), F32),
        jax.ShapeDtypeStruct((TEN, R, 512), F32),
    )
    raw = pl.pallas_call(
        kernel,
        out_shape=results,
        in_specs=[pl.BlockSpec(memory_space=pltpu.SMEM)] + [anywhere] * 10,
        out_specs=(anywhere,) * 4,
        scratch_shapes=[
            pltpu.VMEM((TOK, WIDE), BF16),
            pltpu.VMEM((TOK, WIDE), BF16),
            pltpu.VMEM((TOK, D), BF16),
            pltpu.VMEM((KV, 2, TOK, HEAD), BF16),
            pltpu.VMEM((KV, 2, TOK, HEAD), BF16),
            pltpu.VMEM((2, 4, 1024), F32),
            pltpu.VMEM((8, 2, 4, TOK), F32),
            pltpu.VMEM((2, 1, TOK), jnp.int32),
            pltpu.VMEM((TEN, R, 64), BF16),
            pltpu.VMEM((TEN, R, 512), BF16),
            pltpu.VMEM((2 * TOK, TOK), F32),
            pltpu.VMEM((KV, 2, TOK, HEAD), F32),
            pltpu.VMEM((KV, 2, TOK, HEAD), BF16),
            pltpu.VMEM((KV, 2, TOK, HEAD), BF16),
            pltpu.VMEM((WIDE, TOK), BF16),
            pltpu.VMEM((8, 2, R, 128), BF16),
            pltpu.VMEM((4, 4, 4, R, 128), BF16),
            pltpu.VMEM((4, 8, R, 128), BF16),
            pltpu.VMEM((4, R, 128), BF16),
            pltpu.VMEM((2, 4, 4, R, 128), BF16),
            pltpu.VMEM((2, 4, 4, 2, R, 128), BF16),
            pltpu.VMEM((4, 4, R, 128), BF16),
            pltpu.VMEM((4, 4, 2, R, 128), BF16),
            pltpu.VMEM((4, 4, R, 128), BF16),
            pltpu.VMEM((4, 4, 2, R, 128), BF16),
            pltpu.VMEM((3, 4, R, 128), BF16),
            pltpu.VMEM((3, 4, 2, R, 128), BF16),
            pltpu.VMEM((4, R, 128), BF16),
            pltpu.VMEM((4, 2, R, 128), BF16),
            pltpu.VMEM((3, R, 128), BF16),
            pltpu.VMEM((3, 2, R, 128), BF16),
            pltpu.VMEM((R, 128), BF16),
            pltpu.VMEM((2, R, 128), BF16),
            pltpu.VMEM((3, R, 128), BF16),
            pltpu.VMEM((3, R, 128), BF16),
            pltpu.VMEM((4, 4, R, 128), BF16),
            pltpu.VMEM((4, R, 128), BF16),
            pltpu.VMEM((1, TOK, KV * HEAD), BF16),
            pltpu.VMEM((1, TOK, KV * HEAD), BF16),
            pltpu.VMEM((TEN, R, 64), F32),
            pltpu.VMEM((TEN, R, 512), F32),
            pltpu.SemaphoreType.DMA((N_LOC,)),
            pltpu.SemaphoreType.DMA((N_SEM,)),
            pltpu.SemaphoreType.DMA((N_SEM,)),
        ],
        compiler_params=pltpu.CompilerParams(
            collective_id=0, has_side_effects=True, vmem_limit_bytes=60 * 1024 * 1024
        ),
        cost_estimate=pl.CostEstimate(flops=1_500_000_000, bytes_accessed=5_000_000, transcendentals=1_048_576),
    )(
        tenants, queries, keys, values, output_gradient, layer_input, saved_log_total, row_dot_products, segment_ids,
        jnp.swapaxes(adapter_down, 1, 2), adapter_up,
    )
    key_grad, value_grad, down_grad, up_grad = pl.pallas_call(
        hand_over,
        out_shape=results,
        in_specs=[anywhere] * 4,
        out_specs=(anywhere,) * 4,
        scratch_shapes=[pltpu.VMEM(r.shape, r.dtype) for r in results] + [pltpu.SemaphoreType.DMA((2, 4))],
        compiler_params=pltpu.CompilerParams(vmem_limit_bytes=60 * 1024 * 1024),
        cost_estimate=pl.CostEstimate(flops=0, bytes_accessed=1_000_000, transcendentals=0),
    )(*raw)
    return key_grad, value_grad, jnp.swapaxes(down_grad, 1, 2), up_grad


def solution(mesh):
    tokens = P("dp", ("blk", "uly"), None)
    rows = P("dp", "uly", "blk")
    return jax.shard_map(
        local,
        mesh=mesh,
        in_specs=(
            tokens, tokens, tokens, tokens, tokens, rows, rows, P("dp", None), P("dp"),
            P(None, ("blk", "uly"), None), P(None, None, "uly"),
        ),
        out_specs=(tokens, tokens, P(None, ("blk", "uly"), None), P(None, None, "uly")),
        check_vma=False,
    )
```

time: 1200 us -> 68 us (0.06)
  the two profiles are of different devices: /device:TPU:4 before, /device:TPU:2 now
where the time goes in v1:
time: 68 us; the launch traced here: 67.9 us
  Pallas kernels  66.6 us (98%)
  between operations  1.29 us (2%)
    pallas_call x1, Pallas kernels, local(): pl.pallas_call(kernel, out_shape=results, in_specs=[pl.BlockSpec(memory_s...  64.8 us
    pallas_call x1, Pallas kernels, local(): pl.pallas_call(hand_over, out_shape=results, in_specs=[anywhere] * 4, out...  1.77 us

profile of v1, /device:TPU:2, one launch (start us, length us, event | category | flops | bytes accessed | tf_op | source)
XLA Modules:
  0.0 67.9 jit_solution(15582709276213293187)
XLA Ops:
  1.3 64.8 %shard_map.138 = (bf16[1,128,512]{2,1,0:T(8,128)(2,1)}, bf16[1,128,512]{2,1,0:T(8,128)(2,1)}, f32[4,16,64]{2,1,0:T(8,128)}, f32[4,16,512]{2,1,0:T(8,128)}) custom-call(s32[1]{0:T(128)S(6)} %copy.15.ten_s, bf16[1,128,4096]{2,1,0:T(8,128)(2,1)} %q_h.1, bf16[1,128,512]{2,1,0:T(8,128)(2,1)} %k_h.1, bf16[1,128,512]{2,1,0:T(8,128)(2,1)} %v_h.1, ...), custom_call_target="tpu_custom_call" | custom-call | flops 1500000000 | bytes 5000000 | tf_op jit(solution)/shard_map/pallas_call | solution.py:353
  66.1 1.8 %shard_map.139 = (bf16[1,128,512]{2,1,0:T(8,128)(2,1)}, bf16[1,128,512]{2,1,0:T(8,128)(2,1)}, f32[4,16,64]{2,1,0:T(8,128)}, f32[4,16,512]{2,1,0:T(8,128)}) custom-call(bf16[1,128,512]{2,1,0:T(8,128)(2,1)} %get-tuple-element.12.refs_0_, bf16[1,128,512]{2,1,0:T(8,128)(2,1)} %get-tuple-element.13.refs_1_, f32[4,16,64]{2,1,0:T(8,128)} %get-tuple-element.14.refs_2_, ...), custom_call_target="tpu_custom_call" | custom-call | bytes 1000000 | tf_op jit(solution)/shard_map/pallas_call | solution.py:412

commit v2 on v1

--- a/solution.py
+++ b/solution.py
@@ -223,7 +223,8 @@
     for i in range(KV):
         kv_copies[i].wait_recv()
         one_head(i)
-        go(dkv_copies[i])
+        if i < 2:
+            go(dkv_copies[i])
 
     for copy in u3:
         copy.wait_recv()
@@ -256,10 +257,6 @@
                 s1d[1, n, j, m] = jnp.where(left, pltpu.roll(a, 64, 1), d).astype(BF16)
     cd = go(remote(s1d.at[1 - c], rcd, SEM["cd"], other_core))
 
-    cd.wait_recv()
-    s2d[...] = (s1d[c].astype(F32) + rcd[...].astype(F32)).astype(BF16)
-    xd = to_three("xd", lambda to: s2d.at[to], rxd, x, "x_")
-
     for copy in a2:
         copy.wait_recv()
     down_rows = jnp.concatenate([ag[i, j, k] for i in range(4) for j in range(4) for k in range(4)], axis=1)
@@ -270,13 +267,19 @@
             for k in range(4):
                 s1u[j, k, n] = part[:, (j * 4 + k) * 128:(j * 4 + k + 1) * 128].astype(BF16)
     cu = go(remote(s1u.at[1 - c], rcu, SEM["cu"], other_core))
-    s3d[...] = sum_of_four(s2d[x], rxd, xd)
-    zhd = to_three("zhd", lambda to: s3d.at[to], rhd, zh, "zh_")
+
+    cd.wait_recv()
+    s2d[...] = (s1d[c].astype(F32) + rcd[...].astype(F32)).astype(BF16)
+    xd = to_three("xd", lambda to: s2d.at[to], rxd, x, "x_")
     cu.wait_recv()
     s2u[...] = (s1u[c].astype(F32) + rcu[...].astype(F32)).astype(BF16)
     xu = to_three("xu", lambda to: s2u.at[to], rxu, x, "x_")
+    go(dkv_copies[2])
+    s3d[...] = sum_of_four(s2d[x], rxd, xd)
+    zhd = to_three("zhd", lambda to: s3d.at[to], rhd, zh, "zh_")
     s3u[...] = sum_of_four(s2u[x], rxu, xu)
     zhu = to_three("zhu", lambda to: s3u.at[to], rhu, zh, "zh_")
+    go(dkv_copies[3])
     s4d[...] = sum_of_four(s3d[zh], rhd, zhd)
     zld = to_three("zld", lambda to: s4d.at[div(to, 2)], rld, zl, "zl_")
     s4u[...] = sum_of_four(s3u[zh], rhu, zhu)

time: 68 us -> 67.6 us (level)
  no operation moved by 1% of the time
where the time goes in v2:
time: 67.6 us; the launch traced here: 67.4 us
  Pallas kernels  66.1 us (98%)
  between operations  1.29 us (2%)
    pallas_call x1, Pallas kernels, local(): pl.pallas_call(kernel, out_shape=results, in_specs=[pl.BlockSpec(memory_s...  64.4 us
    pallas_call x1, Pallas kernels, local(): pl.pallas_call(hand_over, out_shape=results, in_specs=[anywhere] * 4, out...  1.77 us

profile of v2, /device:TPU:2, one launch (start us, length us, event | category | flops | bytes accessed | tf_op | source)
XLA Modules:
  0.0 67.4 jit_solution(17482000098403005329)
XLA Ops:
  1.3 64.4 %shard_map.138 = (bf16[1,128,512]{2,1,0:T(8,128)(2,1)}, bf16[1,128,512]{2,1,0:T(8,128)(2,1)}, f32[4,16,64]{2,1,0:T(8,128)}, f32[4,16,512]{2,1,0:T(8,128)}) custom-call(s32[1]{0:T(128)S(6)} %copy.15.ten_s, bf16[1,128,4096]{2,1,0:T(8,128)(2,1)} %q_h.1, bf16[1,128,512]{2,1,0:T(8,128)(2,1)} %k_h.1, bf16[1,128,512]{2,1,0:T(8,128)(2,1)} %v_h.1, ...), custom_call_target="tpu_custom_call" | custom-call | flops 1500000000 | bytes 5000000 | tf_op jit(solution)/shard_map/pallas_call | solution.py:356
  65.7 1.8 %shard_map.139 = (bf16[1,128,512]{2,1,0:T(8,128)(2,1)}, bf16[1,128,512]{2,1,0:T(8,128)(2,1)}, f32[4,16,64]{2,1,0:T(8,128)}, f32[4,16,512]{2,1,0:T(8,128)}) custom-call(bf16[1,128,512]{2,1,0:T(8,128)(2,1)} %get-tuple-element.12.refs_0_, bf16[1,128,512]{2,1,0:T(8,128)(2,1)} %get-tuple-element.13.refs_1_, f32[4,16,64]{2,1,0:T(8,128)} %get-tuple-element.14.refs_2_, ...), custom_call_target="tpu_custom_call" | custom-call | bytes 1000000 | tf_op jit(solution)/shard_map/pallas_call | solution.py:415

commit v3 on v2

--- a/solution.py
+++ b/solution.py
@@ -135,16 +135,6 @@
     au[u, 0] = dot(down_sel.astype(BF16), shift, NN).astype(BF16)
     au[u, 1] = up_sel.astype(BF16)
     ld_all[u] = ld_v[:, :, pl.ds(pl.multiple_of(u * TOK, TOK), TOK)]
-    row = lax.broadcasted_iota(jnp.int32, (TOK, TOK), 0)
-    col = lax.broadcasted_iota(jnp.int32, (TOK, TOK), 1)
-    ids_now = jnp.broadcast_to(seg_v[1].astype(F32), (TOK, TOK))
-    ids_before = jnp.broadcast_to(seg_v[0].astype(F32), (TOK, TOK))
-    now_rows = jnp.sum(jnp.where(row == col, ids_now, 0.0), axis=1, keepdims=True)
-    before_rows = jnp.sum(jnp.where(row == col, ids_before, 0.0), axis=1, keepdims=True)
-    first = jnp.broadcast_to(t, (TOK, TOK)) > 0
-    bias_v[:TOK] = jnp.where((row > col) & (before_rows == ids_now) & first, 0.0, -1e30)
-    bias_v[TOK:] = jnp.where((row <= col) & (now_rows == ids_now), 0.0, -1e30)
-
     for copy in kv_loads:
         copy.wait()
     pl.semaphore_wait(barrier, len(peers))
@@ -171,6 +161,16 @@
     tens = [
         go(remote(ten_v.at[y], ten_v.at[y], SEM["ten"] + k - 1, dev(y_=mod(y + k, 4)))) for k in (1, 2, 3)
     ]
+
+    row = lax.broadcasted_iota(jnp.int32, (TOK, TOK), 0)
+    col = lax.broadcasted_iota(jnp.int32, (TOK, TOK), 1)
+    ids_now = jnp.broadcast_to(seg_v[1].astype(F32), (TOK, TOK))
+    ids_before = jnp.broadcast_to(seg_v[0].astype(F32), (TOK, TOK))
+    now_rows = jnp.sum(jnp.where(row == col, ids_now, 0.0), axis=1, keepdims=True)
+    before_rows = jnp.sum(jnp.where(row == col, ids_before, 0.0), axis=1, keepdims=True)
+    first = jnp.broadcast_to(t, (TOK, TOK)) > 0
+    bias_v[:TOK] = jnp.where((row > col) & (before_rows == ids_now) & first, 0.0, -1e30)
+    bias_v[TOK:] = jnp.where((row <= col) & (now_rows == ids_now), 0.0, -1e30)
 
     for copy in au_copies:
         copy.wait_recv()

time: 67.6 us -> 67.6 us (level)
  no operation moved by 1% of the time
where the time goes in v3:
time: 67.6 us; the launch traced here: 67.4 us
  Pallas kernels  66.1 us (98%)
  between operations  1.29 us (2%)
    pallas_call x1, Pallas kernels, local(): pl.pallas_call(kernel, out_shape=results, in_specs=[pl.BlockSpec(memory_s...  64.4 us
    pallas_call x1, Pallas kernels, local(): pl.pallas_call(hand_over, out_shape=results, in_specs=[anywhere] * 4, out...  1.77 us

profile of v3, /device:TPU:2, one launch (start us, length us, event | category | flops | bytes accessed | tf_op | source)
XLA Modules:
  0.0 67.4 jit_solution(11886222488527206431)
XLA Ops:
  1.3 64.4 %shard_map.138 = (bf16[1,128,512]{2,1,0:T(8,128)(2,1)}, bf16[1,128,512]{2,1,0:T(8,128)(2,1)}, f32[4,16,64]{2,1,0:T(8,128)}, f32[4,16,512]{2,1,0:T(8,128)}) custom-call(s32[1]{0:T(128)S(6)} %copy.15.ten_s, bf16[1,128,4096]{2,1,0:T(8,128)(2,1)} %q_h.1, bf16[1,128,512]{2,1,0:T(8,128)(2,1)} %k_h.1, bf16[1,128,512]{2,1,0:T(8,128)(2,1)} %v_h.1, ...), custom_call_target="tpu_custom_call" | custom-call | flops 1500000000 | bytes 5000000 | tf_op jit(solution)/shard_map/pallas_call | solution.py:356
  65.7 1.8 %shard_map.139 = (bf16[1,128,512]{2,1,0:T(8,128)(2,1)}, bf16[1,128,512]{2,1,0:T(8,128)(2,1)}, f32[4,16,64]{2,1,0:T(8,128)}, f32[4,16,512]{2,1,0:T(8,128)}) custom-call(bf16[1,128,512]{2,1,0:T(8,128)(2,1)} %get-tuple-element.12.refs_0_, bf16[1,128,512]{2,1,0:T(8,128)(2,1)} %get-tuple-element.13.refs_1_, f32[4,16,64]{2,1,0:T(8,128)} %get-tuple-element.14.refs_2_, ...), custom_call_target="tpu_custom_call" | custom-call | bytes 1000000 | tf_op jit(solution)/shard_map/pallas_call | solution.py:415
